TPU v7x, 32 devices: a whole 2x2x4 slice. The times are simulated.
32 devices in a mesh: ctx: 16 (over z, x, core), head: 2 (over y).
Axes of the slice: x: 2, y: 2, z: 4, core: 2. Of those that a mesh axis runs over, the one named last changes fastest.
Arguments:
- query_head_rows: bfloat16 [4096, 4096], P('ctx', 'head'), may hold values from -4 to 4
- key_head_rows: bfloat16 [4096, 1024], P('ctx', 'head'), may hold values from -4 to 4
- value_head_rows: bfloat16 [4096, 1024], P('ctx', 'head'), may hold values from -4 to 4
- forward_output: bfloat16 [4096, 4096], P('ctx', 'head'), may hold values from -4 to 4, as said below
- cotangent: bfloat16 [4096, 4096], P('ctx', 'head'), may hold values from -6 to 6
- logsumexp: float32 [32, 4096], P('head', 'ctx'), as said below
- document_lengths: int32 [16], replicated, may hold values from 1 to 768, as said below
- linear_row_index: int32 [4096], replicated, may hold values from 0 to 4095, as said below
Outputs:
- query_gradient: bfloat16 [4096, 4096], P(('ctx', 'head'))
- linear_key_gradient: bfloat16 [4096, 1024], P(('ctx', 'head'))
- linear_value_gradient: bfloat16 [4096, 1024], P(('ctx', 'head'))
Inputs may be any that keep to these rules, and one draw needn't show every extreme that they name: `logsumexp`: for each head and position, the log of the sum of exp(scores) over the keys that the position sees, from the forward pass on these query_head_rows and key_head_rows. `forward_output`: for each head, the forward pass's softmax weights times value_head_rows, rounded to bfloat16. `document_lengths`: the lengths sum to 4096; the longest document has exactly 768 tokens. `linear_row_index`: A permutation of the 4096 positions. Counting positions in blocks of 256, from one block of the packed sequence at most 32 rows go to one block of linear positions, some pair of blocks reaches 32, and every linear block receives 256 rows.
All inputs are finite; a program needn't handle non-finite values.
Results may differ from a plain program's by a relative error of at most 0.0049.
Values may be sent and summed in bfloat16 or wider, within the bound.
A program may use at most 64 MiB of HBM per device.

v0:
```python
import jax
import jax.numpy as jnp
from jax import lax
from jax.sharding import PartitionSpec as P

HEAD_SIZE = 128
DOC_BLOCKS = 3


def from_behind(shard, axis, by):
    count = lax.axis_size(axis)
    pairs = [(i, i + by) for i in range(count) if 0 <= i + by < count]
    return lax.ppermute(shard, axis, pairs)


def shifted(block, axis, distance):
    devices = range(lax.axis_size(axis))
    route = [((i - distance) % len(devices), i) for i in devices]
    return lax.ppermute(block, axis, route)


def block_grads(
    query_vectors,
    output_gradient,
    log_normalizer,
    row_correction,
    begins,
    query_pos,
    key_part,
    value_part,
    key_start,
):
    length = query_vectors.shape[0]
    kv_heads = query_vectors.shape[1]
    scaling = HEAD_SIZE ** (-0.5)
    key_heads = key_part.reshape(length, kv_heads, HEAD_SIZE)
    value_heads = value_part.reshape(length, kv_heads, HEAD_SIZE)
    scores = (
        jnp.einsum("qngd,knd->qngk", query_vectors, key_heads, preferred_element_type=jnp.float32)
        * scaling
    )
    key_pos = key_start + lax.iota(jnp.int32, length)
    visible = (key_pos[None, :] <= query_pos[:, None]) & (key_pos[None, :] >= begins[:, None])
    weights = jnp.exp(
        jnp.where(visible[:, None, None, :], scores - log_normalizer[..., None], -jnp.inf)
    )
    weights_low = weights.astype(jnp.bfloat16)
    grad_weights = jnp.einsum(
        "qngd,knd->qngk", output_gradient, value_heads, preferred_element_type=jnp.float32
    )
    grad_scores = (weights * (grad_weights - row_correction[..., None]) * scaling).astype(
        jnp.bfloat16
    )
    query_term = jnp.einsum(
        "qngk,knd->qngd", grad_scores, key_heads, preferred_element_type=jnp.float32
    )
    key_term = jnp.einsum(
        "qngk,qngd->knd", grad_scores, query_vectors, preferred_element_type=jnp.float32
    )
    value_term = jnp.einsum(
        "qngk,qngd->knd", weights_low, output_gradient, preferred_element_type=jnp.float32
    )
    return (query_term, key_term.reshape(length, -1), value_term.reshape(length, -1))


def per_device(
    query_head_rows,
    key_head_rows,
    value_head_rows,
    forward_output,
    cotangent,
    logsumexp,
    document_lengths,
    linear_row_index,
):
    length = query_head_rows.shape[0]
    kv_heads = key_head_rows.shape[1] // HEAD_SIZE
    query_groups = logsumexp.shape[0] // kv_heads
    block_index = lax.axis_index("ctx")
    blocks = lax.axis_size("ctx")
    query_pos = block_index * length + lax.iota(jnp.int32, length)
    finish = jnp.cumsum(document_lengths)
    firsts = finish - document_lengths
    begins = jnp.max(jnp.where(firsts[None, :] <= query_pos[:, None], firsts[None, :], 0), axis=1)
    query_vectors = query_head_rows.reshape(length, kv_heads, query_groups, HEAD_SIZE)
    output_gradient = cotangent.reshape(length, kv_heads, query_groups, HEAD_SIZE)
    log_normalizer = logsumexp.T.reshape(length, kv_heads, query_groups)
    row_correction = jnp.sum(
        output_gradient.astype(jnp.float32)
        * forward_output.reshape(length, kv_heads, query_groups, HEAD_SIZE).astype(jnp.float32),
        axis=3,
    )

    def block_terms(key_part, value_part, distance):
        key_start = (block_index - distance) * length

        def compute(operands):
            return block_grads(
                query_vectors,
                output_gradient,
                log_normalizer,
                row_correction,
                begins,
                query_pos,
                operands[0],
                operands[1],
                key_start,
            )

        def nothing(operands):
            empty = jnp.zeros(key_head_rows.shape, jnp.float32)
            return (jnp.zeros(query_vectors.shape, jnp.float32), empty, empty)

        is_live = begins[0] <= key_start + length - 1
        return lax.cond(is_live, compute, nothing, (key_part, value_part))

    query_acc, key_running_sum, value_running_sum = block_terms(key_head_rows, value_head_rows, 0)
    moving_keys, moving_values = (key_head_rows, value_head_rows)
    for distance in range(1, DOC_BLOCKS + 1):
        moving_keys, moving_values = from_behind((moving_keys, moving_values), "ctx", 1)
        key_running_sum, value_running_sum = shifted((key_running_sum, value_running_sum), "ctx", 1)
        query_term, key_term, value_term = block_terms(moving_keys, moving_values, distance)
        query_acc = query_acc + query_term
        key_running_sum = key_running_sum + key_term
        value_running_sum = value_running_sum + value_term
    key_running_sum, value_running_sum = (
        shifted(key_running_sum.astype(jnp.bfloat16), "ctx", -DOC_BLOCKS).astype(
            key_running_sum.dtype
        ),
        shifted(value_running_sum.astype(jnp.bfloat16), "ctx", -DOC_BLOCKS).astype(
            value_running_sum.dtype
        ),
    )
    query_grad = query_acc.reshape(length, -1).astype(jnp.bfloat16)
    key_row_gradient = key_running_sum.astype(jnp.bfloat16)
    value_row_gradient = value_running_sum.astype(jnp.bfloat16)
    capacity = 2 * length // blocks
    own_targets = lax.dynamic_slice_in_dim(linear_row_index, block_index * length, length)
    target = own_targets // length
    owner_marks = (target[:, None] == lax.iota(jnp.int32, blocks)[None, :]).astype(jnp.int32)
    slot_rank = jnp.sum(owner_marks * (jnp.cumsum(owner_marks, axis=0) - 1), axis=1)
    send_slots = target * capacity + slot_rank

    def pack_slots(grad_rows):
        return (
            jnp.zeros((blocks * capacity, grad_rows.shape[1]), grad_rows.dtype)
            .at[send_slots]
            .set(grad_rows)
        )

    arrived = (
        lax.all_to_all(pack_slots(query_grad), "ctx", split_axis=0, concat_axis=0, tiled=True),
        lax.all_to_all(
            pack_slots(key_row_gradient), "ctx", split_axis=0, concat_axis=0, tiled=True
        ),
        lax.all_to_all(
            pack_slots(value_row_gradient), "ctx", split_axis=0, concat_axis=0, tiled=True
        ),
    )
    all_owners = linear_row_index.reshape(blocks, length)
    landing = all_owners // length == block_index
    landed_rank = jnp.cumsum(landing.astype(jnp.int32), axis=1) - 1
    source_slot = lax.iota(jnp.int32, blocks)[:, None] * capacity + landed_rank
    where_to = jnp.where(landing, all_owners % length, length)
    inverse = (
        jnp.zeros((length,), jnp.int32)
        .at[where_to.reshape(-1)]
        .set(source_slot.reshape(-1), mode="drop")
    )
    linear_query = arrived[0][inverse]
    linear_key = arrived[1][inverse]
    linear_value = arrived[2][inverse]
    result = (
        lax.all_to_all(linear_query, "head", split_axis=0, concat_axis=1, tiled=True),
        lax.all_to_all(linear_key, "head", split_axis=0, concat_axis=1, tiled=True),
        lax.all_to_all(linear_value, "head", split_axis=0, concat_axis=1, tiled=True),
    )
    return (result[0], result[1], result[2])


def solution(mesh):
    placed = (
        P("ctx", "head"),
        P("ctx", "head"),
        P("ctx", "head"),
        P("ctx", "head"),
        P("ctx", "head"),
        P("head", "ctx"),
        P(),
        P(),
    )
    return jax.shard_map(
        per_device,
        mesh=mesh,
        in_specs=placed,
        out_specs=(P(("ctx", "head"), None), P(("ctx", "head"), None), P(("ctx", "head"), None)),
        check_vma=False,
    )
```

profile of v0, /device:TPU:10, one launch (start us, length us, event | category | flops | bytes accessed | tf_op | source)
XLA Modules:
  0.0 259.1 jit_solution(17505216491322757662)
XLA Ops:
  3.5 2.3 copy.136
  10.2 11.0 %conditional.4 = (f32[256,512]{0,1:T(8,128)}, f32[256,512]{0,1:T(8,128)}, f32[256,4,4,128]{0,3,2,1:T(8,128)}) conditional(s32[]{:T(128)} %convert_element_type.71, () %tuple.40, (s32[]{:T(128)}, s32[256]{0:T(256)S(1)}, s32[256]{0:T(256)S(1)}, bf16[256,512]{1,0:T(8,128)(2,1)}, bf16[256,4,4,128]{0,3,2,1:T(8,128)(2,1)S(1)}, ...), branch_computations={%region_6.7_spmd, %region_7.8_spmd} | conditional | flops 1353908480 | bytes 36720696 | solution.py:115
  13.2 2.0 fusion.6
  16.7 1.6 fusion.91
  19.3 1.9 copy.218
  21.2 3.6 %collective-permute-start = (bf16[256,512]{1,0:T(8,128)(2,1)}, bf16[256,512]{1,0:T(8,128)(2,1)}, u32[]{:S(2)}, u32[]{:S(2)}) collective-permute-start(bf16[256,512]{1,0:T(8,128)(2,1)} %param.17), channel_id=1, source_target_pairs={{0,2},{2,4},{4,6},{6,8},{8,10},{10,12},{12,14},{14,16},{16,18},{18... | collective-permute-start | bytes 786440 | tf_op jit(solution)/shard_map/ppermute | solution.py:13
  24.7 1.9 collective-permute-start.1
  27.3 5.6 %collective-permute-done = bf16[256,512]{1,0:T(8,128)(2,1)} collective-permute-done((bf16[256,512]{1,0:T(8,128)(2,1)}, bf16[256,512]{1,0:T(8,128)(2,1)}, u32[]{:S(2)}, u32[]{:S(2)}) %collective-permute-start) | collective-permute-done | bytes 262176 | tf_op jit(solution)/shard_map/ppermute | solution.py:13
  32.9 2.8 %collective-permute-done.1 = bf16[256,512]{1,0:T(8,128)(2,1)} collective-permute-done((bf16[256,512]{1,0:T(8,128)(2,1)}, bf16[256,512]{1,0:T(8,128)(2,1)}, u32[]{:S(2)}, u32[]{:S(2)}) %collective-permute-start.1) | collective-permute-done | bytes 262176 | tf_op jit(solution)/shard_map/ppermute | solution.py:13
  35.7 10.8 %conditional.5 = (f32[256,512]{0,1:T(8,128)}, f32[256,512]{0,1:T(8,128)}, f32[256,4,4,128]{0,3,2,1:T(8,128)}) conditional(s32[]{:T(128)} %convert_element_type.75, () %tuple.42, (s32[]{:T(128)}, s32[256]{0:T(256)S(1)}, s32[256]{0:T(256)S(1)}, bf16[256,512]{1,0:T(8,128)(2,1)}, bf16[256,4,4,128]{0,3,2,1:T(8,128)(2,1)S(1)}, ...), branch_computations={%region_8.9_spmd, %region_9.10_spmd} | conditional | flops 1353908480 | bytes 36720696 | solution.py:115
  38.7 1.9 fusion.24
  42.1 1.6 fusion.92
  44.7 1.8 copy.220
  46.5 2.1 add.158
  48.6 4.5 %collective-permute-start.2 = (bf16[256,512]{1,0:T(8,128)(2,1)}, bf16[256,512]{1,0:T(8,128)(2,1)}, u32[]{:S(2)}, u32[]{:S(2)}) collective-permute-start(bf16[256,512]{1,0:T(8,128)(2,1)} %collective-permute-done), channel_id=1, source_target_pairs={{0,2},{2,4},{4,6},{6,8},{8,10},{10,12},{12,14},{14,16},{16,18},{18... | collective-permute-start | bytes 786440 | tf_op jit(solution)/shard_map/ppermute | solution.py:13
  53.0 2.1 collective-permute-start.3
  56.5 3.8 %collective-permute-done.2 = bf16[256,512]{1,0:T(8,128)(2,1)} collective-permute-done((bf16[256,512]{1,0:T(8,128)(2,1)}, bf16[256,512]{1,0:T(8,128)(2,1)}, u32[]{:S(2)}, u32[]{:S(2)}) %collective-permute-start.2) | collective-permute-done | bytes 262176 | tf_op jit(solution)/shard_map/ppermute | solution.py:13
  60.3 2.8 %collective-permute-done.3 = bf16[256,512]{1,0:T(8,128)(2,1)} collective-permute-done((bf16[256,512]{1,0:T(8,128)(2,1)}, bf16[256,512]{1,0:T(8,128)(2,1)}, u32[]{:S(2)}, u32[]{:S(2)}) %collective-permute-start.3) | collective-permute-done | bytes 262176 | tf_op jit(solution)/shard_map/ppermute | solution.py:13
  63.1 3.3 %conditional.6 = (f32[256,512]{0,1:T(8,128)}, f32[256,512]{0,1:T(8,128)}, f32[256,4,4,128]{0,3,2,1:T(8,128)}) conditional(s32[]{:T(128)} %convert_element_type.76, () %tuple.44, (s32[]{:T(128)}, s32[256]{0:T(256)S(1)}, s32[256]{0:T(256)S(1)}, bf16[256,512]{1,0:T(8,128)(2,1)}, bf16[256,4,4,128]{0,3,2,1:T(8,128)(2,1)S(1)}, ...), branch_computations={%region_10.11_spmd, %region_11.12_spmd} | conditional | flops 1353908480 | bytes 36720696 | solution.py:115
  64.8 1.5 broadcast.268.clone
  66.4 2.1 add.159
  68.7 5.3 %collective-permute-start.4 = (bf16[256,512]{1,0:T(8,128)(2,1)}, bf16[256,512]{1,0:T(8,128)(2,1)S(1)}, u32[]{:S(2)}, u32[]{:S(2)}) collective-permute-start(bf16[256,512]{1,0:T(8,128)(2,1)} %collective-permute-done.2), channel_id=1, source_target_pairs={{0,2},{2,4},{4,6},{6,8},{8,10},{10,12},{12,14},{14,16},{16,18},{18... | collective-permute-start | bytes 786440 | tf_op jit(solution)/shard_map/ppermute | solution.py:13
  74.0 1.9 collective-permute-start.5
  76.5 2.1 add.161
  80.1 2.8 %collective-permute-done.5 = bf16[256,512]{1,0:T(8,128)(2,1)S(1)} collective-permute-done((bf16[256,512]{1,0:T(8,128)(2,1)}, bf16[256,512]{1,0:T(8,128)(2,1)S(1)}, u32[]{:S(2)}, u32[]{:S(2)}) %collective-permute-start.5) | collective-permute-done | bytes 262176 | tf_op jit(solution)/shard_map/ppermute | solution.py:13
  82.9 1.6 conditional.7
  83.0 1.6 broadcast.272.clone
  85.7 8.9 %collective-permute-start.9 = (bf16[256,512]{0,1:T(8,128)(2,1)S(1)}, bf16[256,512]{0,1:T(8,128)(2,1)S(1)}, u32[]{:S(2)}, u32[]{:S(2)}) collective-permute-start(bf16[256,512]{0,1:T(8,128)(2,1)S(1)} %add_convert_fusion.2), channel_id=1, source_target_pairs={{6,0},{8,2},{10,4},{12,6},{14,8},{16,10},{18,12},{20,14},{22,16},{... | collective-permute-start | bytes 786440 | tf_op jit(solution)/shard_map/ppermute | solution.py:19
  95.9 9.9 %collective-permute-start.12 = (f32[256,512]{0,1:T(8,128)S(1)}, f32[256,512]{0,1:T(8,128)S(1)}, u32[]{:S(2)}, u32[]{:S(2)}) collective-permute-start(f32[256,512]{0,1:T(8,128)S(1)} %add.162), channel_id=1, source_target_pairs={{30,0},{0,2},{2,4},{4,6},{6,8},{8,10},{10,12},{12,14},{14,16},{16,... | collective-permute-start | bytes 1572872 | tf_op jit(solution)/shard_map/ppermute | solution.py:19
  106.1 2.3 scatter_custom_fusion.2
  108.4 12.3 %all-to-all-start.2 = ((bf16[16,32,512]{2,1,0:T(8,128)(2,1)}), bf16[16,32,512]{2,1,0:T(8,128)(2,1)S(1)}, u32[]{:S(2)}, u32[]{:S(2)}) async-start(bf16[16,32,512]{2,1,0:T(8,128)(2,1)} %bitcast.71), calls=%async_computation.2 | async-start | bytes 1048576 | tf_op jit(solution)/shard_map/all_to_all | solution.py:153
  121.2 18.6 %collective-permute-done.13 = bf16[256,512]{0,1:T(8,128)(2,1)S(1)} collective-permute-done((bf16[256,512]{0,1:T(8,128)(2,1)S(1)}, bf16[256,512]{0,1:T(8,128)(2,1)S(1)}, u32[]{:S(2)}, u32[]{:S(2)}) %collective-permute-start.13) | collective-permute-done | bytes 262176 | tf_op jit(solution)/shard_map/ppermute | solution.py:19
  139.9 2.4 scatter_custom_fusion.3
  142.3 4.2 %all-to-all-start.4 = ((bf16[16,32,512]{2,1,0:T(8,128)(2,1)}), bf16[16,32,512]{2,1,0:T(8,128)(2,1)S(1)}, u32[]{:S(2)}, u32[]{:S(2)}) async-start(bf16[16,32,512]{2,1,0:T(8,128)(2,1)} %bitcast.75), calls=%async_computation.4 | async-start | bytes 1048576 | tf_op jit(solution)/shard_map/all_to_all | solution.py:156
  147.5 15.5 %scatter_custom_fusion.1 = s32[256]{0:T(256)S(1)} fusion(s32[4096]{0:T(1024)S(1)} %compare_select_fusion, s32[4096]{0:T(1024)S(1)} %add.156, s32[]{:T(128)} %constant.107.clone.1), kind=kCustom, calls=%fused_computation.146 | custom fusion | bytes 1028 | tf_op jit(solution)/shard_map/scatter | solution.py:168
  163.1 1.9 gather_fusion.1
  164.9 3.4 %all-to-all-start.3 = ((bf16[2,128,512]{2,1,0:T(8,128)(2,1)}), bf16[2,128,512]{2,1,0:T(8,128)(2,1)S(1)}, u32[]{:S(2)}, u32[]{:S(2)}) async-start(bf16[2,128,512]{2,1,0:T(8,128)(2,1)} %bitcast.73), calls=%async_computation.3 | async-start | bytes 524288 | tf_op jit(solution)/shard_map/all_to_all | solution.py:175
  168.4 4.1 %add_convert_fusion = bf16[256,4,4,128]{0,3,2,1:T(8,128)(2,1)S(1)} fusion(f32[256,4,4,128]{0,3,2,1:T(8,128)} %get-tuple-element.138, f32[256,4,4,128]{0,3,2,1:T(8,128)} %get-tuple-element.137, f32[256,4,4,128]{0,3,2,1:T(8,128)} %get-tuple-element.135, f32[256,4,4,128]{0,3,2,1:T(8,128)} %get-tuple-element.136), kind=kLoop, calls=%fused_computation.95 | loop fusion | flops 2097152 | bytes 9437184 | tf_op jit(solution)/shard_map/convert_element_type | solution.py:134
  173.2 3.7 %scatter_custom_fusion = bf16[512,2048]{1,0:T(8,128)(2,1)} fusion(s32[256]{0:T(256)S(1)} %compare_select_fusion.2, bf16[256,2048]{1,0:T(8,128)(2,1)S(1)} %copy.142, bf16[]{:T(256)} %constant.103.clone.1), kind=kCustom, calls=%fused_computation.97 | custom fusion | bytes 2097154 | tf_op jit(solution)/shard_map/scatter | solution.py:148
  176.9 6.0 %all-to-all-start = ((bf16[16,32,2048]{2,1,0:T(8,128)(2,1)}), bf16[16,32,2048]{2,1,0:T(8,128)(2,1)S(1)}, u32[]{:S(2)}, u32[]{:S(2)}) async-start(bf16[16,32,2048]{2,1,0:T(8,128)(2,1)} %bitcast.236), calls=%async_computation | async-start | bytes 4194304 | tf_op jit(solution)/shard_map/all_to_all | solution.py:152
  182.9 1.9 gather_fusion.2
  184.8 45.4 %all-to-all-done = bf16[16,32,2048]{2,1,0:T(8,128)(2,1)S(1)} async-done(((bf16[16,32,2048]{2,1,0:T(8,128)(2,1)}), bf16[16,32,2048]{2,1,0:T(8,128)(2,1)S(1)}, u32[]{:S(2)}, u32[]{:S(2)}) %all-to-all-start) | async-done | bytes 2097184 | tf_op jit(solution)/shard_map/all_to_all | solution.py:152
  230.2 4.1 %all-to-all-start.5 = ((bf16[2,128,512]{2,1,0:T(8,128)(2,1)}), bf16[2,128,512]{2,1,0:T(8,128)(2,1)}, u32[]{:S(2)}, u32[]{:S(2)}) async-start(bf16[2,128,512]{2,1,0:T(8,128)(2,1)} %bitcast.77), calls=%async_computation.5 | async-start | bytes 524288 | tf_op jit(solution)/shard_map/all_to_all | solution.py:176
  234.3 2.3 gather_fusion
  236.6 3.9 %all-to-all-done.5 = bf16[2,128,512]{2,1,0:T(8,128)(2,1)} async-done(((bf16[2,128,512]{2,1,0:T(8,128)(2,1)}), bf16[2,128,512]{2,1,0:T(8,128)(2,1)}, u32[]{:S(2)}, u32[]{:S(2)}) %all-to-all-start.5) | async-done | bytes 262176 | tf_op jit(solution)/shard_map/all_to_all | solution.py:176
  240.6 3.6 %all-to-all-start.1 = ((bf16[2,128,2048]{2,1,0:T(8,128)(2,1)}), bf16[2,128,2048]{2,1,0:T(8,128)(2,1)S(1)}, u32[]{:S(2)}, u32[]{:S(2)}) async-start(bf16[2,128,2048]{2,1,0:T(8,128)(2,1)} %bitcast.69), calls=%async_computation.1 | async-start | bytes 2097152 | tf_op jit(solution)/shard_map/all_to_all | solution.py:174
  244.9 1.7 copy.228
  246.6 11.4 %all-to-all-done.1 = bf16[2,128,2048]{2,1,0:T(8,128)(2,1)S(1)} async-done(((bf16[2,128,2048]{2,1,0:T(8,128)(2,1)}), bf16[2,128,2048]{2,1,0:T(8,128)(2,1)S(1)}, u32[]{:S(2)}, u32[]{:S(2)}) %all-to-all-start.1) | async-done | bytes 1048608 | tf_op jit(solution)/shard_map/all_to_all | solution.py:174
  (86 shorter events, 28.4 us)
Async XLA Ops:
  5.7 4.5 %copy-start.6 = (f32[16,256]{1,0:T(8,128)S(1)}, f32[16,256]{1,0:T(8,128)}, u32[]{:S(2)}) copy-start(f32[16,256]{1,0:T(8,128)} %param.21) | copy-start | bytes 49156
  10.2 3.0 %copy-start = (bf16[256,4,4,128]{0,3,2,1:T(8,128)(2,1)S(1)}, bf16[256,4,4,128]{0,3,2,1:T(8,128)(2,1)}, u32[]{:S(2)}) copy-start(bf16[256,4,4,128]{0,3,2,1:T(8,128)(2,1)} %get-tuple-element.79) | copy-start | bytes 3145732 | tf_op jit(solution)/shard_map/cond
  21.2 25.3 %collective-permute-start.6 = (f32[256,512]{0,1:T(8,128)}, f32[256,512]{0,1:T(8,128)}, u32[]{:S(2)}, u32[]{:S(2)}) collective-permute-start(f32[256,512]{0,1:T(8,128)} %get-tuple-element.127), channel_id=1, source_target_pairs={{30,0},{0,2},{2,4},{4,6},{6,8},{8,10},{10,12},{12,14},{14,16},{16,... | collective-permute-start | bytes 1572872 | tf_op jit(solution)/shard_map/ppermute | solution.py:19
  21.2 11.7 %collective-permute-start = (bf16[256,512]{1,0:T(8,128)(2,1)}, bf16[256,512]{1,0:T(8,128)(2,1)}, u32[]{:S(2)}, u32[]{:S(2)}) collective-permute-start(bf16[256,512]{1,0:T(8,128)(2,1)} %param.17), channel_id=1, source_target_pairs={{0,2},{2,4},{4,6},{6,8},{8,10},{10,12},{12,14},{14,16},{16,18},{18... | collective-permute-start | bytes 786440 | tf_op jit(solution)/shard_map/ppermute | solution.py:13
  24.7 11.0 %collective-permute-start.1 = (bf16[256,512]{1,0:T(8,128)(2,1)}, bf16[256,512]{1,0:T(8,128)(2,1)}, u32[]{:S(2)}, u32[]{:S(2)}) collective-permute-start(bf16[256,512]{1,0:T(8,128)(2,1)} %param.18), channel_id=1, source_target_pairs={{0,2},{2,4},{4,6},{6,8},{8,10},{10,12},{12,14},{14,16},{16,18},{18... | collective-permute-start | bytes 786440 | tf_op jit(solution)/shard_map/ppermute | solution.py:13
  35.7 3.0 %copy-start.1 = (bf16[256,4,4,128]{0,3,2,1:T(8,128)(2,1)S(1)}, bf16[256,4,4,128]{0,3,2,1:T(8,128)(2,1)}, u32[]{:S(2)}) copy-start(bf16[256,4,4,128]{0,3,2,1:T(8,128)(2,1)} %get-tuple-element.88) | copy-start | bytes 3145732 | tf_op jit(solution)/shard_map/cond
  48.6 17.8 %collective-permute-start.7 = (f32[256,512]{0,1:T(8,128)}, f32[256,512]{0,1:T(8,128)}, u32[]{:S(2)}, u32[]{:S(2)}) collective-permute-start(f32[256,512]{0,1:T(8,128)} %add.158), channel_id=1, source_target_pairs={{30,0},{0,2},{2,4},{4,6},{6,8},{8,10},{10,12},{12,14},{14,16},{16,... | collective-permute-start | bytes 1572872 | tf_op jit(solution)/shard_map/ppermute | solution.py:19
  48.6 11.7 %collective-permute-start.2 = (bf16[256,512]{1,0:T(8,128)(2,1)}, bf16[256,512]{1,0:T(8,128)(2,1)}, u32[]{:S(2)}, u32[]{:S(2)}) collective-permute-start(bf16[256,512]{1,0:T(8,128)(2,1)} %collective-permute-done), channel_id=1, source_target_pairs={{0,2},{2,4},{4,6},{6,8},{8,10},{10,12},{12,14},{14,16},{16,18},{18... | collective-permute-start | bytes 786440 | tf_op jit(solution)/shard_map/ppermute | solution.py:13
  53.0 10.1 %collective-permute-start.3 = (bf16[256,512]{1,0:T(8,128)(2,1)}, bf16[256,512]{1,0:T(8,128)(2,1)}, u32[]{:S(2)}, u32[]{:S(2)}) collective-permute-start(bf16[256,512]{1,0:T(8,128)(2,1)} %collective-permute-done.1), channel_id=1, source_target_pairs={{0,2},{2,4},{4,6},{6,8},{8,10},{10,12},{12,14},{14,16},{16,18},{18... | collective-permute-start | bytes 786440 | tf_op jit(solution)/shard_map/ppermute | solution.py:13
  55.1 21.3 %collective-permute-start.10 = (f32[256,512]{0,1:T(8,128)}, f32[256,512]{0,1:T(8,128)}, u32[]{:S(2)}, u32[]{:S(2)}) collective-permute-start(f32[256,512]{0,1:T(8,128)} %get-tuple-element.131), channel_id=1, source_target_pairs={{30,0},{0,2},{2,4},{4,6},{6,8},{8,10},{10,12},{12,14},{14,16},{16,... | collective-permute-start | bytes 1572872 | tf_op jit(solution)/shard_map/ppermute | solution.py:19
  63.1 5.5 %copy-start.7 = (s32[4096]{0:T(1024)S(1)}, s32[4096]{0:T(1024)}, u32[]{:S(2)}) copy-start(s32[4096]{0:T(1024)} %param.23) | copy-start | bytes 49156
  68.5 16.1 %collective-permute-start.8 = (f32[256,512]{0,1:T(8,128)}, f32[256,512]{0,1:T(8,128)}, u32[]{:S(2)}, u32[]{:S(2)}) collective-permute-start(f32[256,512]{0,1:T(8,128)} %add.159), channel_id=1, source_target_pairs={{30,0},{0,2},{2,4},{4,6},{6,8},{8,10},{10,12},{12,14},{14,16},{16,... | collective-permute-start | bytes 1572872 | tf_op jit(solution)/shard_map/ppermute | solution.py:19
  68.7 11.5 %collective-permute-start.4 = (bf16[256,512]{1,0:T(8,128)(2,1)}, bf16[256,512]{1,0:T(8,128)(2,1)S(1)}, u32[]{:S(2)}, u32[]{:S(2)}) collective-permute-start(bf16[256,512]{1,0:T(8,128)(2,1)} %collective-permute-done.2), channel_id=1, source_target_pairs={{0,2},{2,4},{4,6},{6,8},{8,10},{10,12},{12,14},{14,16},{16,18},{18... | collective-permute-start | bytes 786440 | tf_op jit(solution)/shard_map/ppermute | solution.py:13
  74.0 9.0 %collective-permute-start.5 = (bf16[256,512]{1,0:T(8,128)(2,1)}, bf16[256,512]{1,0:T(8,128)(2,1)S(1)}, u32[]{:S(2)}, u32[]{:S(2)}) collective-permute-start(bf16[256,512]{1,0:T(8,128)(2,1)} %collective-permute-done.3), channel_id=1, source_target_pairs={{0,2},{2,4},{4,6},{6,8},{8,10},{10,12},{12,14},{14,16},{16,18},{18... | collective-permute-start | bytes 786440 | tf_op jit(solution)/shard_map/ppermute | solution.py:13
  78.6 16.1 %collective-permute-start.11 = (f32[256,512]{0,1:T(8,128)}, f32[256,512]{0,1:T(8,128)}, u32[]{:S(2)}, u32[]{:S(2)}) collective-permute-start(f32[256,512]{0,1:T(8,128)} %add.161), channel_id=1, source_target_pairs={{30,0},{0,2},{2,4},{4,6},{6,8},{8,10},{10,12},{12,14},{14,16},{16,... | collective-permute-start | bytes 1572872 | tf_op jit(solution)/shard_map/ppermute | solution.py:19
  85.7 20.2 %collective-permute-start.9 = (bf16[256,512]{0,1:T(8,128)(2,1)S(1)}, bf16[256,512]{0,1:T(8,128)(2,1)S(1)}, u32[]{:S(2)}, u32[]{:S(2)}) collective-permute-start(bf16[256,512]{0,1:T(8,128)(2,1)S(1)} %add_convert_fusion.2), channel_id=1, source_target_pairs={{6,0},{8,2},{10,4},{12,6},{14,8},{16,10},{18,12},{20,14},{22,16},{... | collective-permute-start | bytes 786440 | tf_op jit(solution)/shard_map/ppermute | solution.py:19
  95.9 24.8 %collective-permute-start.12 = (f32[256,512]{0,1:T(8,128)S(1)}, f32[256,512]{0,1:T(8,128)S(1)}, u32[]{:S(2)}, u32[]{:S(2)}) collective-permute-start(f32[256,512]{0,1:T(8,128)S(1)} %add.162), channel_id=1, source_target_pairs={{30,0},{0,2},{2,4},{4,6},{6,8},{8,10},{10,12},{12,14},{14,16},{16,... | collective-permute-start | bytes 1572872 | tf_op jit(solution)/shard_map/ppermute | solution.py:19
  108.4 33.9 %all-to-all-start.2 = ((bf16[16,32,512]{2,1,0:T(8,128)(2,1)}), bf16[16,32,512]{2,1,0:T(8,128)(2,1)S(1)}, u32[]{:S(2)}, u32[]{:S(2)}) async-start(bf16[16,32,512]{2,1,0:T(8,128)(2,1)} %bitcast.71), calls=%async_computation.2 | async-start | bytes 1048576 | tf_op jit(solution)/shard_map/all_to_all | solution.py:153
  120.8 19.0 %collective-permute-start.13 = (bf16[256,512]{0,1:T(8,128)(2,1)S(1)}, bf16[256,512]{0,1:T(8,128)(2,1)S(1)}, u32[]{:S(2)}, u32[]{:S(2)}) collective-permute-start(bf16[256,512]{0,1:T(8,128)(2,1)S(1)} %add_convert_fusion.1), channel_id=1, source_target_pairs={{6,0},{8,2},{10,4},{12,6},{14,8},{16,10},{18,12},{20,14},{22,16},{... | collective-permute-start | bytes 786440 | tf_op jit(solution)/shard_map/ppermute | solution.py:19
  142.3 22.7 %all-to-all-start.4 = ((bf16[16,32,512]{2,1,0:T(8,128)(2,1)}), bf16[16,32,512]{2,1,0:T(8,128)(2,1)S(1)}, u32[]{:S(2)}, u32[]{:S(2)}) async-start(bf16[16,32,512]{2,1,0:T(8,128)(2,1)} %bitcast.75), calls=%async_computation.4 | async-start | bytes 1048576 | tf_op jit(solution)/shard_map/all_to_all | solution.py:156
  164.9 12.0 %all-to-all-start.3 = ((bf16[2,128,512]{2,1,0:T(8,128)(2,1)}), bf16[2,128,512]{2,1,0:T(8,128)(2,1)S(1)}, u32[]{:S(2)}, u32[]{:S(2)}) async-start(bf16[2,128,512]{2,1,0:T(8,128)(2,1)} %bitcast.73), calls=%async_computation.3 | async-start | bytes 524288 | tf_op jit(solution)/shard_map/all_to_all | solution.py:175
  176.9 53.3 %all-to-all-start = ((bf16[16,32,2048]{2,1,0:T(8,128)(2,1)}), bf16[16,32,2048]{2,1,0:T(8,128)(2,1)S(1)}, u32[]{:S(2)}, u32[]{:S(2)}) async-start(bf16[16,32,2048]{2,1,0:T(8,128)(2,1)} %bitcast.236), calls=%async_computation | async-start | bytes 4194304 | tf_op jit(solution)/shard_map/all_to_all | solution.py:152
  230.2 10.4 %all-to-all-start.5 = ((bf16[2,128,512]{2,1,0:T(8,128)(2,1)}), bf16[2,128,512]{2,1,0:T(8,128)(2,1)}, u32[]{:S(2)}, u32[]{:S(2)}) async-start(bf16[2,128,512]{2,1,0:T(8,128)(2,1)} %bitcast.77), calls=%async_computation.5 | async-start | bytes 524288 | tf_op jit(solution)/shard_map/all_to_all | solution.py:176
  240.6 17.4 %all-to-all-start.1 = ((bf16[2,128,2048]{2,1,0:T(8,128)(2,1)}), bf16[2,128,2048]{2,1,0:T(8,128)(2,1)S(1)}, u32[]{:S(2)}, u32[]{:S(2)}) async-start(bf16[2,128,2048]{2,1,0:T(8,128)(2,1)} %bitcast.69), calls=%async_computation.1 | async-start | bytes 2097152 | tf_op jit(solution)/shard_map/all_to_all | solution.py:174
where the time goes:
time: 257 us; the launch traced here: 259 us
  waiting for transfers between devices  97.8 us (38%)
  starting transfers between devices  72.9 us (28%)
  local copies, waits for them, and re-layouts  54.2 us (21%)
  other arithmetic  17.2 us (7%)
  matrix products  13.4 us (5%)
  between operations  3.5 us (1%)
    all_to_all x1, waiting for transfers between devices, per_device(): lax.all_to_all(pack_slots(query_grad), 'ctx', split_axis=0, concat_axis=0...  45.4 us
    ppermute x8, starting transfers between devices, shifted(): return lax.ppermute(block, axis, route)  20 us
    ppermute x6, starting transfers between devices, from_behind(): return lax.ppermute(shard, axis, pairs)  19.2 us
    ppermute x8, waiting for transfers between devices, shifted(): return lax.ppermute(block, axis, route)  18.6 us
    ppermute x6, waiting for transfers between devices, from_behind(): return lax.ppermute(shard, axis, pairs)  18.4 us
    scatter x1, local copies, waits for them, and re-layouts, per_device(): inverse = jnp.zeros((length,), jnp.int32).at[where_to.reshape(-1)].set(so...  15.5 us
    all_to_all x1, starting transfers between devices, per_device(): lax.all_to_all(pack_slots(key_row_gradient), 'ctx', split_axis=0, concat_...  12.3 us
    all_to_all x1, waiting for transfers between devices, per_device(): lax.all_to_all(linear_query, 'head', split_axis=0, concat_axis=1, tiled=T...  11.4 us
  transfers between devices with their start and end apart: 20, of which 10 were waited for; matrix products, arithmetic and copies ran while one was open for 24% of the time, Pallas kernels for 0%

commit v1 on v0

v1 whole, which is shorter than its diff:
```python
import functools

import jax
import jax.numpy as jnp
from jax import lax
from jax.experimental import pallas as pl
from jax.experimental.pallas import tpu as pltpu
from jax.sharding import PartitionSpec as P

HEAD_SIZE = 128
DOC_BLOCKS = 3
MESH = pl.DeviceIdType.MESH
NT = (((1,), (1,)), ((), ()))
TN = (((0,), (0,)), ((), ()))
LOG2E = 1.4426950408889634


def kernel(
    blocks,
    heads,
    cap,
    q_ref,
    k_ref,
    v_ref,
    o_ref,
    do_ref,
    lse_ref,
    lens_ref,
    lri_ref,
    outq_ref,
    outk_ref,
    outv_ref,
    kv_in,
    bias,
    send_pick,
    land_t,
    land_pick,
    part_out,
    part_in,
    own_part,
    q_out,
    q_in,
    kv_out,
    kv_back,
    hq,
    hkv,
    kv_ssem,
    kv_rsem,
    part_ssem,
    part_rsem,
    row_ssem,
    row_rsem,
    head_ssem,
    head_rsem,
):
    length, d = q_ref.shape[0], HEAD_SIZE
    kv_heads = k_ref.shape[1] // d
    width = q_ref.shape[1] // kv_heads
    groups = width // d
    kv_cols = kv_heads * d
    slots = blocks * cap
    out_rows = length // heads
    scale = d**-0.5
    me = lax.axis_index("ctx")
    my_head = lax.axis_index("head")
    f32, bf16 = jnp.float32, jnp.bfloat16

    def peer(by):
        return lax.rem(me + by + blocks, blocks)

    barrier = pltpu.get_barrier_semaphore()

    def greet(s, _):
        pl.semaphore_signal(barrier, inc=1, device_id=(peer(s), my_head), device_id_type=MESH)
        return 0

    def greet_head(s, _):
        pl.semaphore_signal(
            barrier, inc=1, device_id=(me, lax.rem(my_head + s, heads)), device_id_type=MESH
        )
        return 0

    lax.fori_loop(1, blocks, greet, 0)
    lax.fori_loop(1, heads, greet_head, 0)
    pl.semaphore_wait(barrier, blocks - 1 + heads - 1)

    def cols(n, size):
        return pl.ds(pl.multiple_of(n * size, size), size)

    def kv_copy(n, dist, which):
        source = (k_ref, v_ref)[which]
        return pltpu.make_async_remote_copy(
            src_ref=source.at[:, cols(n, d)],
            dst_ref=kv_in.at[n, dist - 1, which],
            send_sem=kv_ssem.at[n, dist - 1, which],
            recv_sem=kv_rsem.at[n, dist - 1, which],
            device_id=(peer(dist), my_head),
            device_id_type=MESH,
        )

    def part_copy(n, dist, which):
        return pltpu.make_async_remote_copy(
            src_ref=part_out.at[n, dist - 1, which],
            dst_ref=part_in.at[n, dist - 1, which],
            send_sem=part_ssem.at[n, dist - 1, which],
            recv_sem=part_rsem.at[n, dist - 1, which],
            device_id=(peer(-dist), my_head),
            device_id_type=MESH,
        )

    def slot_rows(block):
        return pl.ds(pl.multiple_of(block * cap, cap), cap)

    def row_copy(stage, s, dst_block):
        to = peer(s)
        if stage is None:
            src, dst, index = kv_out, kv_back, kv_heads
        else:
            src, dst, index = q_out.at[stage], q_in.at[stage], stage
        return pltpu.make_async_remote_copy(
            src_ref=src.at[slot_rows(to), :],
            dst_ref=dst.at[slot_rows(dst_block), :],
            send_sem=row_ssem.at[index, s],
            recv_sem=row_rsem.at[index, s],
            device_id=(to, my_head),
            device_id_type=MESH,
        )

    def head_copies(stage, s, dst_head):
        to = lax.rem(my_head + s, heads)
        rows = pl.ds(pl.multiple_of(to * out_rows, out_rows), out_rows)
        if stage is None:
            triples = (
                (hkv.at[rows, :kv_cols], outk_ref.at[:, cols(dst_head, kv_cols)], kv_heads),
                (hkv.at[rows, kv_cols:], outv_ref.at[:, cols(dst_head, kv_cols)], kv_heads + 1),
            )
        else:
            triples = (
                (hq.at[stage, rows, :], outq_ref.at[:, cols(dst_head * kv_heads + stage, width)], stage),
            )
        return [
            pltpu.make_async_remote_copy(
                src_ref=src,
                dst_ref=dst,
                send_sem=head_ssem.at[index, s],
                recv_sem=head_rsem.at[index, s],
                device_id=(me, to),
                device_id_type=MESH,
            )
            for src, dst, index in triples
        ]

    def start_kv(n, _):
        for dist in range(1, DOC_BLOCKS + 1):
            for which in range(2):
                kv_copy(n, dist, which).start()
        return 0

    lax.fori_loop(0, kv_heads, start_kv, 0)

    q_pos = me * length + lax.broadcasted_iota(jnp.int32, (1, length), 1)
    begins = jnp.zeros((1, length), jnp.int32)
    first = jnp.int32(0)
    for i in range(lens_ref.shape[0]):
        begins = jnp.where(q_pos >= first, jnp.maximum(begins, first), begins)
        first = first + lens_ref[i]
    for dist in range(DOC_BLOCKS + 1):
        k_pos = (me - dist) * length + lax.broadcasted_iota(jnp.int32, (length, length), 0)
        seen = (k_pos <= q_pos) & (k_pos >= begins)
        bias[dist] = jnp.where(seen, 0.0, -jnp.inf).astype(f32)

    before = (
        lax.broadcasted_iota(jnp.int32, (length, length), 0)
        <= lax.broadcasted_iota(jnp.int32, (length, length), 1)
    ).astype(f32).astype(bf16)
    mine = lri_ref[pl.ds(me, 1), :]
    block_start = length * lax.broadcasted_iota(jnp.int32, (blocks, length), 0)
    owner = ((mine >= block_start) & (mine < block_start + length)).astype(f32)
    counts = jnp.dot(owner.astype(bf16), before, preferred_element_type=f32)
    block_base = (cap * lax.broadcasted_iota(jnp.int32, (blocks, length), 0)).astype(f32)
    slot = jnp.sum(owner * (block_base + counts - 1.0), axis=0, keepdims=True)
    slot_ids = lax.broadcasted_iota(jnp.int32, (slots, length), 0).astype(f32)
    send_pick[...] = (slot_ids == slot).astype(f32).astype(bf16)
    all_rows = lri_ref[...]
    base = me * length
    landing = ((all_rows >= base) & (all_rows < base + length)).astype(f32)
    landed = jnp.dot(landing.astype(bf16), before, preferred_element_type=f32)
    rank = jnp.where(landing > 0.5, landed - 1.0, -1.0)
    place_ids = lax.broadcasted_iota(jnp.int32, (length, length), 0)
    rank_ids = lax.broadcasted_iota(jnp.int32, (cap, length), 0).astype(f32)
    for i in range(blocks):
        at_place = (place_ids == all_rows[i : i + 1] - base).astype(f32).astype(bf16)
        at_rank = (rank_ids == rank[i : i + 1]).astype(f32).astype(bf16)
        land_t[i * cap : (i + 1) * cap, :] = lax.dot_general(
            at_rank, at_place, NT, preferred_element_type=f32
        )
    land_pick[...] = jnp.transpose(land_t[...]).astype(bf16)

    def start_rows(stage):
        def body(s, _):
            row_copy(stage, s, me).start()
            return 0

        lax.fori_loop(1, blocks, body, 0)

    def head_group(n, _):
        def stack(ref):
            return jnp.concatenate(
                [
                    ref[:, pl.ds(pl.multiple_of(n * width + g * d, d), d)]
                    for g in range(groups)
                ],
                axis=0,
            )

        qs, dos = stack(q_ref), stack(do_ref)
        product = dos.astype(f32) * stack(o_ref).astype(f32)
        delta = lax.dot_general(
            jnp.ones((8, d), f32),
            product,
            NT,
            precision=lax.Precision.HIGHEST,
            preferred_element_type=f32,
        )[0:1]
        lse2 = lse_ref[n] * LOG2E
        dq = None
        for dist in range(DOC_BLOCKS + 1):
            if dist == 0:
                kd, vd = k_ref[:, cols(n, d)], v_ref[:, cols(n, d)]
            else:
                for which in range(2):
                    kv_copy(n, dist, which).wait_recv()
                kd, vd = kv_in[n, dist - 1, 0], kv_in[n, dist - 1, 1]
            scores = lax.dot_general(kd, qs, NT, preferred_element_type=f32)
            mask = jnp.concatenate([bias[dist]] * groups, axis=1)
            weights = jnp.exp2(scores * (scale * LOG2E) - lse2 + mask)
            grad_w = lax.dot_general(vd, dos, NT, preferred_element_type=f32)
            grad_s = (weights * (grad_w - delta) * scale).astype(bf16)
            dv = jnp.dot(weights.astype(bf16), dos, preferred_element_type=f32)
            dk = jnp.dot(grad_s, qs, preferred_element_type=f32)
            term = lax.dot_general(grad_s, kd, TN, preferred_element_type=f32)
            dq = term if dq is None else dq + term
            if dist == 0:
                own_part[n, 0] = dk
                own_part[n, 1] = dv
            else:
                part_out[n, dist - 1, 0] = dk.astype(bf16)
                part_out[n, dist - 1, 1] = dv.astype(bf16)
                for which in range(2):
                    part_copy(n, dist, which).start()
        dq = dq.astype(bf16)
        for g in range(groups):
            q_out[n, :, g * d : (g + 1) * d] = jnp.dot(
                send_pick[...], dq[g * length : (g + 1) * length], preferred_element_type=f32
            ).astype(bf16)
        start_rows(n)
        return 0

    lax.fori_loop(0, kv_heads, head_group, 0)

    for n in range(kv_heads):
        for which in range(2):
            total = own_part[n, which]
            for dist in range(1, DOC_BLOCKS + 1):
                part_copy(n, dist, which).wait_recv()
                total = total + part_in[n, dist - 1, which].astype(f32)
            at = which * kv_cols + n * d
            kv_out[:, at : at + d] = jnp.dot(
                send_pick[...], total.astype(bf16), preferred_element_type=f32
            ).astype(bf16)
    start_rows(None)

    my_rows = pl.ds(pl.multiple_of(my_head * out_rows, out_rows), out_rows)

    def finish_rows(stage):
        def body(s, _):
            row_copy(stage, s, peer(-s)).wait_recv()
            return 0

        lax.fori_loop(1, blocks, body, 0)
        if stage is None:
            kv_back[slot_rows(me), :] = kv_out[slot_rows(me), :]
            hkv[...] = jnp.dot(
                land_pick[...], kv_back[...], preferred_element_type=f32
            ).astype(bf16)
        else:
            q_in[stage, slot_rows(me), :] = q_out[stage, slot_rows(me), :]
            hq[stage] = jnp.dot(
                land_pick[...], q_in[stage], preferred_element_type=f32
            ).astype(bf16)

        def send(s, _):
            for copy in head_copies(stage, s, my_head):
                copy.start()
            return 0

        lax.fori_loop(1, heads, send, 0)
        if stage is None:
            outk_ref[:, cols(my_head, kv_cols)] = hkv[my_rows, :kv_cols]
            outv_ref[:, cols(my_head, kv_cols)] = hkv[my_rows, kv_cols:]
        else:
            outq_ref[:, cols(my_head * kv_heads + stage, width)] = hq[stage, my_rows, :]

    def finish_q(n, _):
        finish_rows(n)
        return 0

    lax.fori_loop(0, kv_heads, finish_q, 0)
    finish_rows(None)

    def settle(stage):
        def arrive(s, _):
            for copy in head_copies(stage, s, lax.rem(my_head - s + heads, heads)):
                copy.wait_recv()
                copy.wait_send()
            return 0

        def sent(s, _):
            row_copy(stage, s, me).wait_send()
            return 0

        lax.fori_loop(1, heads, arrive, 0)
        lax.fori_loop(1, blocks, sent, 0)

    def settle_q(n, _):
        settle(n)
        for dist in range(1, DOC_BLOCKS + 1):
            for which in range(2):
                kv_copy(n, dist, which).wait_send()
                part_copy(n, dist, which).wait_send()
        return 0

    lax.fori_loop(0, kv_heads, settle_q, 0)
    settle(None)


def per_device(
    blocks,
    heads,
    query_head_rows,
    key_head_rows,
    value_head_rows,
    forward_output,
    cotangent,
    logsumexp,
    document_lengths,
    linear_row_index,
):
    length, q_cols = query_head_rows.shape
    kv_cols = key_head_rows.shape[1]
    d = HEAD_SIZE
    n = kv_cols // d
    width = q_cols // n
    cap = max(16, 2 * length // blocks)
    slots = blocks * cap
    rows = length // heads
    bf16, f32 = jnp.bfloat16, jnp.float32
    vmem = pl.BlockSpec(memory_space=pltpu.VMEM)
    dma = pltpu.SemaphoreType.DMA
    return pl.pallas_call(
        functools.partial(kernel, blocks, heads, cap),
        out_shape=(
            jax.ShapeDtypeStruct((rows, q_cols * heads), bf16),
            jax.ShapeDtypeStruct((rows, kv_cols * heads), bf16),
            jax.ShapeDtypeStruct((rows, kv_cols * heads), bf16),
        ),
        in_specs=[vmem] * 6 + [pl.BlockSpec(memory_space=pltpu.SMEM), vmem],
        out_specs=(vmem,) * 3,
        scratch_shapes=[
            pltpu.VMEM((n, DOC_BLOCKS, 2, length, d), bf16),
            pltpu.VMEM((DOC_BLOCKS + 1, length, length), f32),
            pltpu.VMEM((slots, length), bf16),
            pltpu.VMEM((slots, length), f32),
            pltpu.VMEM((length, slots), bf16),
            pltpu.VMEM((n, DOC_BLOCKS, 2, length, d), bf16),
            pltpu.VMEM((n, DOC_BLOCKS, 2, length, d), bf16),
            pltpu.VMEM((n, 2, length, d), f32),
            pltpu.VMEM((n, slots, width), bf16),
            pltpu.VMEM((n, slots, width), bf16),
            pltpu.VMEM((slots, 2 * kv_cols), bf16),
            pltpu.VMEM((slots, 2 * kv_cols), bf16),
            pltpu.VMEM((n, length, width), bf16),
            pltpu.VMEM((length, 2 * kv_cols), bf16),
            dma((n, DOC_BLOCKS, 2)),
            dma((n, DOC_BLOCKS, 2)),
            dma((n, DOC_BLOCKS, 2)),
            dma((n, DOC_BLOCKS, 2)),
            dma((n + 1, blocks)),
            dma((n + 1, blocks)),
            dma((n + 2, heads)),
            dma((n + 2, heads)),
        ],
        compiler_params=pltpu.CompilerParams(
            collective_id=0, has_side_effects=True, vmem_limit_bytes=56 * 2**20
        ),
    )(
        query_head_rows,
        key_head_rows,
        value_head_rows,
        forward_output,
        cotangent,
        logsumexp.reshape(n, 1, -1),
        document_lengths,
        linear_row_index.reshape(blocks, length),
    )


def solution(mesh):
    placed = (
        P("ctx", "head"),
        P("ctx", "head"),
        P("ctx", "head"),
        P("ctx", "head"),
        P("ctx", "head"),
        P("head", "ctx"),
        P(),
        P(),
    )
    rows = P(("ctx", "head"), None)
    return jax.shard_map(
        functools.partial(per_device, mesh.shape["ctx"], mesh.shape["head"]),
        mesh=mesh,
        in_specs=placed,
        out_specs=(rows, rows, rows),
        check_vma=False,
    )
```

time: 257 us -> 128 us (0.50)
  Pallas kernels: 0 us -> 121 us
  waiting for transfers between devices: 97.8 us -> 0 us
  starting transfers between devices: 72.9 us -> 0 us
  local copies, waits for them, and re-layouts: 54.2 us -> 6.04 us
  other arithmetic: 17.2 us -> 0 us
  matrix products: 13.4 us -> 0 us
  between operations: 3.5 us -> 0.66 us
    pallas_call x0 -> x1, Pallas kernels: none -> 121 us  [per_device(): pl.pallas_call(functools.partial(kernel, blocks, heads, cap), out_shape=(...]
    all_to_all x6 -> x0, waiting for transfers between devices: 60.8 us -> none  [the longest x1 45.4 us: per_device(): lax.all_to_all(pack_slots(query_grad), 'ctx', split_axis=0, concat_axis=0...]
    ppermute x14 -> x0, starting transfers between devices: 39.2 us -> none  [the longest x8 20 us: shifted(): return lax.ppermute(block, axis, route)]
    ppermute x14 -> x0, waiting for transfers between devices: 37 us -> none  [the longest x8 18.6 us: shifted(): return lax.ppermute(block, axis, route)]
    all_to_all x6 -> x0, starting transfers between devices: 33.7 us -> none  [the longest x1 12.3 us: per_device(): lax.all_to_all(pack_slots(key_row_gradient), 'ctx', split_axis=0, concat_...]
    scatter x4 -> x0, local copies, waits for them, and re-layouts: 23.9 us -> none  [the longest x1 15.5 us: per_device(): inverse = jnp.zeros((length,), jnp.int32).at[where_to.reshape(-1)].set(so...]
    dot_general x10 -> x0, matrix products: 13.4 us -> none  [the longest x2 3.92 us: block_grads(): jnp.einsum('qngk,qngd->knd', weights_low, output_gradient, preferred_elem...]
    add x8 -> x0, other arithmetic: 7.54 us -> none  [the longest x2 4.19 us: per_device(): key_running_sum = key_running_sum + key_term]
  transfers between devices with their start and end apart: 20 -> 0, of which waited for: 10 -> 0; matrix products, arithmetic and copies ran while one was open for 24% -> 0% of each run, Pallas kernels for 0% -> 0%
where the time goes in v1:
time: 128 us
  Pallas kernels  121 us (95%)
  local copies, waits for them, and re-layouts  6.04 us (5%)
    pallas_call x1, Pallas kernels, per_device(): pl.pallas_call(functools.partial(kernel, blocks, heads, cap), out_shape=(...  121 us
    unnamed x9, local copies, waits for them, and re-layouts  4.08 us

profile of v1, /device:TPU:10, one launch (start us, length us, event | category | flops | bytes accessed | tf_op | source)
XLA Modules:
  0.0 128.1 jit_solution(6446636764330513178)
XLA Ops:
  0.6 0.0 copy-start.2
  0.6 1.3 %reshape.12.lse_ref = f32[4,1,1024]{2,1,0:T(1,128)} reshape(f32[16,256]{1,0:T(8,128)} %param.13) | data formatting | bytes 32768 | tf_op jit(solution)/shard_map/reshape | solution.py:402
  2.0 0.0 copy-done.2
  2.0 0.6 reshape.13.lri_ref
  2.6 121.4 %shard_map.103 = (bf16[128,4096]{1,0:T(8,128)(2,1)}, bf16[128,1024]{1,0:T(8,128)(2,1)}, bf16[128,1024]{1,0:T(8,128)(2,1)}) custom-call(bf16[256,2048]{1,0:T(8,128)(2,1)} %q_ref.1, bf16[256,512]{1,0:T(8,128)(2,1)} %k_ref.1, bf16[256,512]{1,0:T(8,128)(2,1)} %v_ref.1, bf16[256,2048]{1,0:T(8,128)(2,1)} %o_ref.1, bf16[256,2048]{1,0:T(8,128)(2,1)} %do_ref.1, ...), custom_call_target="tpu_custom_call" | custom-call | tf_op jit(solution)/shard_map/pallas_call | solution.py:360
  124.0 0.0 copy-start.1
  124.0 2.3 %copy.14 = bf16[128,4096]{1,0:T(8,128)(2,1)} copy(bf16[128,4096]{1,0:T(8,128)(2,1)} %get-tuple-element.6) | data formatting | bytes 2097152
  126.4 0.0 copy-done.1
  126.4 0.0 copy-start
  126.4 0.7 copy.15
  127.1 0.3 copy-done
  127.4 0.7 copy.16
Async XLA Ops:
  0.6 1.4 %copy-start.2 = (s32[4096]{0:T(1024)S(1)}, s32[4096]{0:T(1024)}, u32[]{:S(2)}) copy-start(s32[4096]{0:T(1024)} %param.15) | copy-start | bytes 49156
  124.0 2.3 %copy-start.1 = (bf16[128,1024]{1,0:T(8,128)(2,1)S(1)}, bf16[128,1024]{1,0:T(8,128)(2,1)}, u32[]{:S(2)}) copy-start(bf16[128,1024]{1,0:T(8,128)(2,1)} %get-tuple-element.7) | copy-start | bytes 786436
  126.4 1.0 copy-start
